TPU v7x, 32 devices: a whole 2x2x4 slice. The times are simulated.
32 devices in a mesh: group: 2 (over y), row: 4 (over z), blk: 2 (over x), span: 2 (over core).
Axes of the slice: x: 2, y: 2, z: 4, core: 2. Of those that a mesh axis runs over, the one named last changes fastest.
Arguments:
- adjoint_in: bfloat16 [1024, 10, 32, 256], P('row', 'group', 'blk', 'span'), parts along dimension 1, may hold values from -6 to 6
- stencil_coef: float32 [10, 32, 256], P('group', 'blk', 'span'), parts along dimension 0, may hold values from -0.6 to 0.6
- rotor_lag: float32 [32], P('group'), parts along dimension 0, may hold values from -3.140625 to 3.140625
- stator_lag: float32 [24], P('group'), parts along dimension 0, may hold values from -3.140625 to 3.140625
- rotor_harm: int32 [256], replicated, may hold values from 0 to 15
- stator_harm: int32 [256], replicated, may hold values from 0 to 11
Outputs:
- adjoint_out: bfloat16 [1024, 10, 32, 256], P('row', 'group', 'blk', 'span'), parts along dimension 1
There are 2 independent parts, one for each index of `group`. A program takes and returns all parts, laid end to end along the dimension named above; an argument that names none is the same for every part. Nothing has to cross between parts.
All inputs are finite; a program needn't handle non-finite values.
Results may differ from a plain program's by a relative error of at most 0.0058.
Values may be sent and summed in bfloat16 or wider, within the bound.
A program may use at most 192 MiB of HBM per device.

v0:
```python
import functools
import math

import jax
import jax.numpy as jnp
import numpy as np
from jax import lax
from jax.experimental import pallas as pl
from jax.experimental.pallas import tpu as pltpu
from jax.sharding import PartitionSpec as P

AZ = 1024
MODES = 256
LANES = 128
MESH = pl.DeviceIdType.MESH


def make_table(points, modes_count):
    point_idx = np.arange(points, dtype=np.int64)
    mode_order = np.arange(1, modes_count + 1, dtype=np.int64)
    phase_idx = point_idx[:, None] * mode_order[None, :] % points
    angles = phase_idx.astype(np.float32) * np.float32(2.0 * math.pi / points)
    return np.concatenate([np.cos(angles), np.sin(angles)], axis=1).astype(jnp.bfloat16)


def table_lookup(index_arr, lag_table):
    matches = index_arr[:, None] == jnp.arange(lag_table.shape[0], dtype=jnp.int32)[None, :]
    return jnp.sum(jnp.where(matches, lag_table[None, :], 0.0), axis=1)


def lanes_at(start, size):
    return pl.ds(pl.multiple_of(start, LANES), size)


def kernel(
    states, x_dev, chunk,
    f_ref, coef_ref, scale_ref, analysis_ref, table_ref,
    out_ref,
    gath, stage, ret, local, across, first_x, last_x, coef_got,
    fwd_send, fwd_recv, back_send, back_recv, halo_send, halo_recv,
):
    n = lax.axis_size("row")
    me = lax.axis_index("row")
    blks = lax.axis_size("blk")
    blk = lax.axis_index("blk")
    span = lax.axis_index("span")
    rows, columns = f_ref.shape
    share = columns // n
    chunks = share // chunk
    modes = table_ref.shape[1] // 2
    plane = x_dev * LANES

    peers = [lax.rem(me + off, n) for off in range(1, n)]
    sources = [lax.rem(me + n - off, n) for off in range(1, n)]
    blk_next = lax.rem(blk + 1, blks)
    blk_prev = lax.rem(blk + blks - 1, blks)
    span_other = 1 - span

    barrier = pltpu.get_barrier_semaphore()
    for peer in peers:
        pl.semaphore_signal(barrier, inc=1, device_id={"row": peer}, device_id_type=MESH)
    pl.semaphore_signal(barrier, inc=1, device_id={"blk": blk_next}, device_id_type=MESH)
    pl.semaphore_signal(barrier, inc=1, device_id={"blk": blk_prev}, device_id_type=MESH)
    pl.semaphore_signal(barrier, inc=1, device_id={"span": span_other}, device_id_type=MESH)
    pl.semaphore_wait(barrier, n + 2)

    def forward(ch, off, peer):
        return pltpu.make_async_remote_copy(
            src_ref=f_ref.at[:, lanes_at(peer * share + ch * chunk, chunk)],
            dst_ref=gath.at[pl.ds(pl.multiple_of(me * rows, 16), rows), lanes_at(ch * chunk, chunk)],
            send_sem=fwd_send.at[ch, off],
            recv_sem=fwd_recv.at[ch, off],
            device_id={"row": peer},
            device_id_type=MESH,
        )

    def backward(ch, off, peer):
        return pltpu.make_async_remote_copy(
            src_ref=stage.at[pl.ds(pl.multiple_of(peer * rows, 16), rows), lanes_at(ch * chunk, chunk)],
            dst_ref=ret.at[:, lanes_at(me * share + ch * chunk, chunk)],
            send_sem=back_send.at[ch, off],
            recv_sem=back_recv.at[ch, off],
            device_id={"row": peer},
            device_id_type=MESH,
        )

    def halo(idx, src, dst, where):
        return pltpu.make_async_remote_copy(
            src_ref=src, dst_ref=dst,
            send_sem=halo_send.at[idx], recv_sem=halo_recv.at[idx],
            device_id=where, device_id_type=MESH,
        )

    halos = [
        halo(0, coef_ref, coef_got.at[0], {"span": span_other}),
        halo(1, coef_ref, coef_got.at[1], {"blk": blk_prev}),
        halo(2, coef_ref, coef_got.at[2], {"blk": blk_next}),
        halo(3, f_ref, across, {"span": span_other}),
    ]
    for c in range(states):
        here = pl.ds(c * LANES, LANES)
        halos.append(halo(4 + 2 * c, f_ref.at[:, pl.ds(c * plane, LANES)], first_x.at[:, here], {"blk": blk_prev}))
        halos.append(
            halo(5 + 2 * c, f_ref.at[:, pl.ds((c + 1) * plane - LANES, LANES)], last_x.at[:, here], {"blk": blk_next})
        )

    @pl.loop(0, chunks)
    def _(ch):
        for off, peer in enumerate(peers):
            forward(ch, off, peer).start()

    for copy in halos:
        copy.start()

    gath[pl.ds(pl.multiple_of(me * rows, 16), rows), :] = f_ref[:, lanes_at(me * share, share)]

    cos_scale = scale_ref[:, 0:1]
    sin_scale = scale_ref[:, 1:2]

    @pl.loop(0, chunks)
    def _(ch):
        for off, peer in enumerate(peers):
            forward(ch, off, peer).wait_recv()
        here = lanes_at(ch * chunk, chunk)
        coeffs = jnp.dot(analysis_ref[...], gath[:, here], preferred_element_type=jnp.float32)
        cos_part = coeffs[:modes]
        sin_part = coeffs[modes:]
        rotated = jnp.concatenate(
            [cos_scale * cos_part + sin_scale * sin_part, cos_scale * sin_part - sin_scale * cos_part], axis=0
        ).astype(jnp.bfloat16)
        synthesis = jnp.dot(table_ref[...], rotated, preferred_element_type=jnp.float32)
        stage[:, here] = (synthesis * (2.0 / AZ)).astype(jnp.bfloat16)
        for off, peer in enumerate(peers):
            backward(ch, off, peer).start()
        ret[:, lanes_at(me * share + ch * chunk, chunk)] = stage[pl.ds(pl.multiple_of(me * rows, 16), rows), here]

    for copy in halos:
        copy.wait_recv()

    step = 64
    lane = lax.broadcasted_iota(jnp.int32, (step, LANES), 1)
    has_next = blk < blks - 1
    has_prev = blk > 0

    @pl.loop(0, states)
    def _(c):
        @pl.loop(0, rows // step)
        def _(rb):
            here = pl.ds(pl.multiple_of(rb * step, step), step)

            def field_at(x):
                return f_ref[here, lanes_at(c * plane + x * LANES, LANES)].astype(jnp.float32)

            def other_at(x):
                return across[here, lanes_at(c * plane + x * LANES, LANES)].astype(jnp.float32)

            def coef_at(k, x):
                return coef_ref[k : k + 1, x * LANES : (x + 1) * LANES]

            edge = lanes_at(c * LANES, LANES)
            before = coef_got[2, 2:3, plane - LANES : plane] * last_x[here, edge].astype(jnp.float32)
            after = coef_got[1, 1:2, 0:LANES] * first_x[here, edge].astype(jnp.float32)
            before = jnp.where(has_prev, before, 0.0)
            after = jnp.where(has_next, after, 0.0)
            now = field_at(0)
            prev_term = before
            for x in range(x_dev):
                later = field_at(x + 1) if x + 1 < x_dev else None
                next_term = coef_at(1, x + 1) * later if later is not None else after
                other = other_at(x)
                cols = slice(x * LANES, (x + 1) * LANES)
                right_edge = jnp.where(span == 0, coef_got[0, 3:4, cols] * other, 0.0)
                left_edge = jnp.where(span == 1, coef_got[0, 4:5, cols] * other, 0.0)
                right = pltpu.roll(jnp.where(lane == 0, right_edge, coef_at(3, x) * now), LANES - 1, 1)
                left = pltpu.roll(jnp.where(lane == LANES - 1, left_edge, coef_at(4, x) * now), 1, 1)
                local[here, lanes_at(c * plane + x * LANES, LANES)] = (
                    coef_at(0, x) * now + next_term + prev_term + right + left
                )
                prev_term = coef_at(2, x) * now
                now = later

    def finish(start):
        cols = lanes_at(start, chunk)
        out_ref[:, cols] = (local[:, cols] + ret[:, cols].astype(jnp.float32)).astype(jnp.bfloat16)

    @pl.loop(0, chunks)
    def _(ch):
        finish(me * share + ch * chunk)

    @pl.loop(0, chunks)
    def _(ch):
        for off, (peer, source) in enumerate(zip(peers, sources)):
            backward(ch, off, peer).wait_recv()
            finish(source * share + ch * chunk)

    @pl.loop(0, chunks)
    def _(ch):
        for off, peer in enumerate(peers):
            forward(ch, off, peer).wait_send()
            backward(ch, off, peer).wait_send()

    for copy in halos:
        copy.wait_send()


def on_device(adjoint_in, stencil_coef, rotor_lag, stator_lag, rotor_harm, stator_harm):
    rows, states, x_dev, s_dev = adjoint_in.shape
    n = lax.axis_size("row")
    columns = states * x_dev * s_dev
    tiles = columns // n // LANES
    chunk = LANES * max(d for d in (1, 2, 4) if tiles % d == 0)
    chunks = columns // n // chunk
    table = make_table(AZ, MODES)
    in_rotor = lax.axis_index("blk") * 2 < lax.axis_size("blk")
    phase_angle = jnp.where(in_rotor, table_lookup(rotor_harm, rotor_lag), table_lookup(stator_harm, stator_lag))
    scale = jnp.stack([jnp.cos(phase_angle), jnp.sin(phase_angle)], axis=1)
    coef = jnp.pad(stencil_coef.reshape(5, x_dev * s_dev), ((0, 3), (0, 0)))
    vmem = pl.BlockSpec(memory_space=pltpu.VMEM)
    dma = pltpu.SemaphoreType.DMA
    out = pl.pallas_call(
        functools.partial(kernel, states, x_dev, chunk),
        out_shape=jax.ShapeDtypeStruct((rows, columns), jnp.bfloat16),
        in_specs=[vmem] * 5,
        out_specs=vmem,
        scratch_shapes=[
            pltpu.VMEM((n * rows, columns // n), jnp.bfloat16),
            pltpu.VMEM((n * rows, columns // n), jnp.bfloat16),
            pltpu.VMEM((rows, columns), jnp.bfloat16),
            pltpu.VMEM((rows, columns), jnp.float32),
            pltpu.VMEM((rows, columns), jnp.bfloat16),
            pltpu.VMEM((rows, states * LANES), jnp.bfloat16),
            pltpu.VMEM((rows, states * LANES), jnp.bfloat16),
            pltpu.VMEM((3, 8, x_dev * s_dev), jnp.float32),
            dma((chunks, n - 1)),
            dma((chunks, n - 1)),
            dma((chunks, n - 1)),
            dma((chunks, n - 1)),
            dma((4 + 2 * states,)),
            dma((4 + 2 * states,)),
        ],
        compiler_params=pltpu.CompilerParams(
            collective_id=0, has_side_effects=True, vmem_limit_bytes=60 * 1024 * 1024
        ),
        name="passage",
    )(
        adjoint_in.reshape(rows, columns),
        coef,
        scale,
        jnp.asarray(np.ascontiguousarray(table.T)),
        jnp.asarray(table),
    )
    return out.reshape(adjoint_in.shape)


def solution(mesh):
    in_specs = (
        P("row", "group", "blk", "span"),
        P("group", "blk", "span"),
        P("group"),
        P("group"),
        P(),
        P(),
    )
    out_specs = P("row", "group", "blk", "span")
    return jax.shard_map(
        on_device, mesh=mesh, in_specs=in_specs, out_specs=out_specs, check_vma=False
    )
```

profile of v0, /device:TPU:10, one launch (start us, length us, event | category | flops | bytes accessed | tf_op | source)
XLA Modules:
  0.0 251.0 jit_solution(9566695502365767359)
XLA Ops:
  0.0 0.8 select_reduce_fusion.1
  0.8 0.8 select_reduce_fusion
  1.6 0.8 copy.19
  2.4 0.6 pad.4.coef_ref
  3.0 0.8 copy.12.scale_ref
  3.8 6.2 %copy.18 = bf16[32,8,80,128]{3,1,2,0:T(8,128)(2,1)} copy(bf16[32,8,80,128]{3,2,1,0:T(8,128)(2,1)} %bitcast.16) | data formatting | bytes 10485760
  10.0 234.9 %passage.1 = bf16[256,10240]{1,0:T(8,128)(2,1)} custom-call(bf16[256,10240]{1,0:T(8,128)(2,1)} %bitcast.15, f32[8,2048]{1,0:T(8,128)} %pad.4.coef_ref, f32[256,2]{1,0:T(8,128)} %copy.12.scale_ref, bf16[512,1024]{1,0:T(8,128)(2,1)} %constant.14.clone.analysis_ref, bf16[1024,512]{1,0:T(8,128)(2,1)} %constant.15.clone.table_ref), custom_call_target="tpu_custom_call" | custom-call | tf_op jit(solution)/shard_map/passage/pallas_call | solution.py:220
  244.9 6.1 %copy.15 = bf16[32,8,80,128]{3,2,1,0:T(8,128)(2,1)} copy(bf16[32,8,80,128]{3,1,2,0:T(8,128)(2,1)} %bitcast.14) | data formatting | bytes 10485760
  (2 shorter events, 0.1 us)
where the time goes:
time: 251 us
  Pallas kernels  235 us (94%)
  local copies, waits for them, and re-layouts  14.5 us (6%)
    pallas_call x1, Pallas kernels, on_device(): pl.pallas_call(functools.partial(kernel, states, x_dev, chunk), out_shape...  235 us
    unnamed x3, local copies, waits for them, and re-layouts  13.1 us

commit v1 on v0

v1 whole, which is shorter than its diff:
```python
import math

import jax
import jax.numpy as jnp
import numpy as np
from jax import lax
from jax.experimental import pallas as pl
from jax.experimental.pallas import tpu as pltpu
from jax.sharding import PartitionSpec as P

AZ = 1024
MODES = 256
LANES = 128
MESH = pl.DeviceIdType.MESH


def make_table(points, modes_count):
    point_idx = np.arange(points, dtype=np.int64)
    mode_order = np.arange(1, modes_count + 1, dtype=np.int64)
    phase_idx = point_idx[:, None] * mode_order[None, :] % points
    angles = phase_idx.astype(np.float32) * np.float32(2.0 * math.pi / points)
    return np.concatenate([np.cos(angles), np.sin(angles)], axis=1).astype(jnp.bfloat16)


def lanes_at(start, size):
    return pl.ds(pl.multiple_of(start, LANES), size)


def rows_at(start, size):
    return pl.ds(pl.multiple_of(start, 16), size)


def kernel(
    rotor_lag, stator_lag, rotor_harm, stator_harm, coef_ref, field_ref, analysis_hbm, table_hbm,
    out_ref,
    slabs, flat, gath, stage, ret, local, across, first_x, last_x, coef_got, lined, analysis, table,
    in_sem, out_sem, table_sem, fwd_send, fwd_recv, back_send, back_recv, coef_send, coef_recv, halo_send, halo_recv,
):
    n = lax.axis_size("row")
    me = lax.axis_index("row")
    blks = lax.axis_size("blk")
    blk = lax.axis_index("blk")
    span = lax.axis_index("span")
    states, rows, x_dev, _ = slabs.shape
    plane = x_dev * LANES
    share = plane // n
    modes = table.shape[1] // 2
    step = min(rows, 64)

    peers = [lax.rem(me + off, n) for off in range(1, n)]
    blk_next = lax.rem(blk + 1, blks)
    blk_prev = lax.rem(blk + blks - 1, blks)
    span_other = 1 - span
    own = rows_at(me * rows, rows)

    def load_slab(c):
        return pltpu.make_async_copy(field_ref.at[:, c], slabs.at[c], in_sem.at[c])

    def store_slab(c):
        return pltpu.make_async_copy(slabs.at[c], out_ref.at[:, c], out_sem.at[c])

    load_tables = [
        pltpu.make_async_copy(analysis_hbm, analysis, table_sem.at[0]),
        pltpu.make_async_copy(table_hbm, table, table_sem.at[1]),
    ]

    @pl.loop(0, states)
    def _(c):
        load_slab(c).start()

    for copy in load_tables:
        copy.start()

    barrier = pltpu.get_barrier_semaphore()
    for peer in peers:
        pl.semaphore_signal(barrier, inc=1, device_id={"row": peer}, device_id_type=MESH)
    pl.semaphore_signal(barrier, inc=1, device_id={"blk": blk_next}, device_id_type=MESH)
    pl.semaphore_signal(barrier, inc=1, device_id={"blk": blk_prev}, device_id_type=MESH)
    pl.semaphore_signal(barrier, inc=1, device_id={"span": span_other}, device_id_type=MESH)

    def remote(src, dst, send_sem, recv_sem, where):
        return pltpu.make_async_remote_copy(
            src_ref=src, dst_ref=dst, send_sem=send_sem, recv_sem=recv_sem, device_id=where, device_id_type=MESH
        )

    def forward(c, off, peer):
        return remote(
            flat.at[c, :, lanes_at(peer * share, share)], gath.at[c, own, :],
            fwd_send.at[c, off], fwd_recv.at[c, off], {"row": peer},
        )

    def backward(c, off, peer):
        return remote(
            stage.at[c, rows_at(peer * rows, rows), :], ret.at[c, :, lanes_at(me * share, share)],
            back_send.at[c, off], back_recv.at[c, off], {"row": peer},
        )

    def halos(c):
        return [
            remote(flat.at[c], across.at[c], halo_send.at[c, 0], halo_recv.at[c, 0], {"span": span_other}),
            remote(
                flat.at[c, :, pl.ds(0, LANES)], first_x.at[c], halo_send.at[c, 1], halo_recv.at[c, 1],
                {"blk": blk_prev},
            ),
            remote(
                flat.at[c, :, pl.ds(plane - LANES, LANES)], last_x.at[c], halo_send.at[c, 2], halo_recv.at[c, 2],
                {"blk": blk_next},
            ),
        ]

    coef_copies = [
        remote(coef_ref, coef_got.at[i], coef_send.at[i], coef_recv.at[i], where)
        for i, where in enumerate(({"span": span_other}, {"blk": blk_prev}, {"blk": blk_next}))
    ]

    def flatten(c):
        @pl.loop(0, rows // step)
        def _(rb):
            here = rows_at(rb * step, step)
            lined[...] = slabs[c, here].astype(jnp.float32).reshape(step * x_dev, LANES)
            for x in range(x_dev):
                flat[c, here, x * LANES : (x + 1) * LANES] = lined[pl.ds(x, step, stride=x_dev), :].astype(jnp.bfloat16)

    load_slab(0).wait()
    flatten(0)
    pl.semaphore_wait(barrier, n + 2)

    @pl.loop(0, states)
    def _(c):
        @pl.when(c > 0)
        def _():
            load_slab(c).wait()
            flatten(c)

        for off, peer in enumerate(peers):
            forward(c, off, peer).start()
        for copy in halos(c):
            copy.start()

    for copy in coef_copies:
        copy.start()

    rotor = jnp.zeros((1, modes), jnp.float32)
    for h in range(rotor_lag.shape[0]):
        rotor = jnp.where(rotor_harm[...] == h, rotor_lag[h], rotor)
    stator = jnp.zeros((1, modes), jnp.float32)
    for h in range(stator_lag.shape[0]):
        stator = jnp.where(stator_harm[...] == h, stator_lag[h], stator)
    angle = jnp.where(blk * 2 < blks, rotor, stator)
    cos_scale = jnp.transpose(jnp.broadcast_to(jnp.cos(angle), (8, modes)))[:, 0:1]
    sin_scale = jnp.transpose(jnp.broadcast_to(jnp.sin(angle), (8, modes)))[:, 0:1]

    for copy in load_tables:
        copy.wait()

    @pl.loop(0, states)
    def _(c):
        gath[c, own, :] = flat[c, :, lanes_at(me * share, share)]
        for off, peer in enumerate(peers):
            forward(c, off, peer).wait_recv()
        coeffs = jnp.dot(analysis[...], gath[c], preferred_element_type=jnp.float32)
        cos_part = coeffs[:modes]
        sin_part = coeffs[modes:]
        rotated = jnp.concatenate(
            [cos_scale * cos_part + sin_scale * sin_part, cos_scale * sin_part - sin_scale * cos_part], axis=0
        ).astype(jnp.bfloat16)
        synthesis = jnp.dot(table[...], rotated, preferred_element_type=jnp.float32)
        stage[c] = (synthesis * (2.0 / AZ)).astype(jnp.bfloat16)
        for off, peer in enumerate(peers):
            backward(c, off, peer).start()
        ret[c, :, lanes_at(me * share, share)] = stage[c, own, :]

    for copy in coef_copies:
        copy.wait_recv()

    lane = lax.broadcasted_iota(jnp.int32, (step, LANES), 1)
    has_next = blk < blks - 1
    has_prev = blk > 0

    @pl.loop(0, states)
    def _(c):
        for copy in halos(c):
            copy.wait_recv()

        @pl.loop(0, rows // step)
        def _(rb):
            here = rows_at(rb * step, step)

            def field_at(x):
                return flat[c, here, x * LANES : (x + 1) * LANES].astype(jnp.float32)

            def coef_at(k, x):
                return coef_ref[k, x : x + 1, :]

            before = coef_got[2, 2, x_dev - 1 : x_dev, :] * last_x[c, here, :].astype(jnp.float32)
            after = coef_got[1, 1, 0:1, :] * first_x[c, here, :].astype(jnp.float32)
            before = jnp.where(has_prev, before, 0.0)
            after = jnp.where(has_next, after, 0.0)
            now = field_at(0)
            prev_term = before
            for x in range(x_dev):
                cols = slice(x * LANES, (x + 1) * LANES)
                later = field_at(x + 1) if x + 1 < x_dev else None
                next_term = coef_at(1, x + 1) * later if later is not None else after
                other = across[c, here, cols].astype(jnp.float32)
                right_edge = jnp.where(span == 0, coef_got[0, 3, x : x + 1, :] * other, 0.0)
                left_edge = jnp.where(span == 1, coef_got[0, 4, x : x + 1, :] * other, 0.0)
                right = pltpu.roll(jnp.where(lane == 0, right_edge, coef_at(3, x) * now), LANES - 1, 1)
                left = pltpu.roll(jnp.where(lane == LANES - 1, left_edge, coef_at(4, x) * now), 1, 1)
                local[c, here, cols] = coef_at(0, x) * now + next_term + prev_term + right + left
                prev_term = coef_at(2, x) * now
                now = later

    @pl.loop(0, states)
    def _(c):
        for off, peer in enumerate(peers):
            backward(c, off, peer).wait_recv()

        @pl.loop(0, rows // step)
        def _(rb):
            here = rows_at(rb * step, step)
            for x in range(x_dev):
                cols = slice(x * LANES, (x + 1) * LANES)
                lined[pl.ds(x, step, stride=x_dev), :] = local[c, here, cols] + ret[c, here, cols].astype(jnp.float32)
            slabs[c, here] = lined[...].reshape(step, x_dev, LANES).astype(jnp.bfloat16)

        store_slab(c).start()

    @pl.loop(0, states)
    def _(c):
        for off, peer in enumerate(peers):
            forward(c, off, peer).wait_send()
            backward(c, off, peer).wait_send()
        for copy in halos(c):
            copy.wait_send()
        store_slab(c).wait()

    for copy in coef_copies:
        copy.wait_send()


def on_device(adjoint_in, stencil_coef, rotor_lag, stator_lag, rotor_harm, stator_harm):
    rows, states, x_dev, s_dev = adjoint_in.shape
    n = lax.axis_size("row")
    table = make_table(AZ, MODES)
    vmem = pl.BlockSpec(memory_space=pltpu.VMEM)
    smem = pl.BlockSpec(memory_space=pltpu.SMEM)
    hbm = pl.BlockSpec(memory_space=pl.ANY)
    dma = pltpu.SemaphoreType.DMA
    share = x_dev * s_dev // n
    field16 = lambda shape: pltpu.VMEM(shape, jnp.bfloat16)
    field32 = lambda shape: pltpu.VMEM(shape, jnp.float32)
    return pl.pallas_call(
        kernel,
        out_shape=jax.ShapeDtypeStruct(adjoint_in.shape, jnp.bfloat16),
        in_specs=[smem, smem, vmem, vmem, vmem, hbm, hbm, hbm],
        out_specs=hbm,
        scratch_shapes=[
            field16((states, rows, x_dev, s_dev)),
            field16((states, rows, x_dev * s_dev)),
            field16((states, n * rows, share)),
            field16((states, n * rows, share)),
            field16((states, rows, x_dev * s_dev)),
            field32((states, rows, x_dev * s_dev)),
            field16((states, rows, x_dev * s_dev)),
            field16((states, rows, s_dev)),
            field16((states, rows, s_dev)),
            field32((3, 5, x_dev, s_dev)),
            field32((min(rows, 64) * x_dev, s_dev)),
            field16((2 * MODES, AZ)),
            field16((AZ, 2 * MODES)),
            dma((states,)),
            dma((states,)),
            dma((2,)),
            dma((states, n - 1)),
            dma((states, n - 1)),
            dma((states, n - 1)),
            dma((states, n - 1)),
            dma((3,)),
            dma((3,)),
            dma((states, 3)),
            dma((states, 3)),
        ],
        compiler_params=pltpu.CompilerParams(
            collective_id=0, has_side_effects=True, vmem_limit_bytes=60 * 1024 * 1024
        ),
        name="passage",
    )(
        rotor_lag,
        stator_lag,
        rotor_harm.reshape(1, MODES),
        stator_harm.reshape(1, MODES),
        stencil_coef,
        adjoint_in,
        jnp.asarray(np.ascontiguousarray(table.T)),
        jnp.asarray(table),
    )


def solution(mesh):
    in_specs = (
        P("row", "group", "blk", "span"),
        P("group", "blk", "span"),
        P("group"),
        P("group"),
        P(),
        P(),
    )
    out_specs = P("row", "group", "blk", "span")
    return jax.shard_map(
        on_device, mesh=mesh, in_specs=in_specs, out_specs=out_specs, check_vma=False
    )
```

time: 251 us -> 239 us (0.952)
  local copies, waits for them, and re-layouts: 14.5 us -> 5.74 us
    unnamed x3 -> x1, local copies, waits for them, and re-layouts: 13.1 us -> 5.74 us
where the time goes in v1:
time: 239 us
  Pallas kernels  233 us (97%)
  local copies, waits for them, and re-layouts  5.74 us (2%)
    pallas_call x1, Pallas kernels, on_device(): pl.pallas_call(kernel, out_shape=jax.ShapeDtypeStruct(adjoint_in.shape, j...  233 us
    unnamed x1, local copies, waits for them, and re-layouts  5.74 us

profile of v1, /device:TPU:10, one launch (start us, length us, event | category | flops | bytes accessed | tf_op | source)
XLA Modules:
  0.0 239.1 jit_solution(17836296782492121765)
XLA Ops:
  0.0 233.4 %passage.1 = bf16[256,5,16,128]{3,2,1,0:T(8,128)(2,1)} custom-call(f32[16]{0:T(128)} %rotor_lag.1, f32[12]{0:T(128)} %stator_lag.1, s32[1,256]{1,0:T(1,128)} %bitcast.2, s32[1,256]{1,0:T(1,128)} %bitcast.3, f32[5,16,128]{2,1,0:T(8,128)} %coef_ref.1, bf16[256,5,16,128]{3,2,1,0:T(8,128)(2,1)} %field_ref.1, bf16[512,1024]{1,0:T(8,128)(2,1)} %constant.4.clone.analysis_hbm, ...), custom_call_target="tpu_custom_call" | custom-call | tf_op jit(solution)/shard_map/passage/pallas_call | solution.py:253
  233.4 5.7 %copy.10 = bf16[256,5,16,128]{3,2,1,0:T(8,128)(2,1)} copy(bf16[256,5,16,128]{3,2,1,0:T(8,128)(2,1)} %passage.1) | data formatting | bytes 10485760
